TPU v7x, 512 devices: a whole 4x8x8 slice. The times are simulated.
512 devices in a mesh: orient: 16 (over y_hi, z), slab: 32 (over x, y_lo, core).
Axes of the slice: x: 4, y: 8 (y_hi: 2, y_lo: 4; y = y_hi * 4 + y_lo), z: 8, core: 2. Of those that a mesh axis runs over, the one named last changes fastest.
Arguments:
- images: bfloat16 [1024, 65536], P('orient', 'slab'), may hold values from -8 to 8
- projections: bfloat16 [8, 768, 65536], P(None, 'orient', 'slab'), may hold values from -0.0234375 to 0.0234375
- noise_weight: float32 [65536], P('slab'), may hold values from 0.5 to 4
- prior_score: float32 [8, 768], P(None, 'orient'), may hold values from -4 to 4
- routing: int32 [32, 768, 16, 2], P('slab', 'orient'), may hold values from 0 to 63, as said below
- insert_kernel: bfloat16 [32, 64, 128, 128], P('slab', 'orient'), may hold values from -1.5 to 1.5
Outputs:
- volume: float32 [32, 64, 8, 128], P('slab', 'orient')
Inputs may be any that keep to these rules, and one draw needn't show every extreme that they name: routing[s, o, p, 0] names the slab owner that receives slice block s * 16 + p of orientation o, and routing[s, o, p, 1] a volume block of that owner's slab, below 64. Among the 768 entries with one s and one aligned block of 48 orientations, no owner is named more than 48 times, and for each aligned block of orientations there is one owner (the same for every s) that is named exactly 48 times for each s.
All inputs are finite; a program needn't handle non-finite values.
Results may differ from a plain program's by a relative error of at most 0.008.
Values may be sent and summed in bfloat16 or wider, within the bound.
No kernel may reach another device: no remote copies, remote signals or barrier semaphores. Data moves between devices by JAX's collectives and lax.ppermute only.
A program may use at most 64 MiB of HBM per device.

v0:
```python
import jax
import jax.numpy as jnp
from jax import lax
from jax.sharding import PartitionSpec as P

PIECE = 128


def joined(value, axis, join):
    pieces = jax.tree.map(lambda part: lax.all_gather(part, axis), value)
    head = jax.tree.map(lambda part: part[0], pieces)
    tail = jax.tree.map(lambda part: part[1:], pieces)
    subtotal, _ = lax.scan(lambda subtotal, slab: (join(subtotal, slab), None), head, tail)
    return subtotal


def combine_totals(earlier, later):
    ceiling = jnp.maximum(earlier[0], later[0])
    return (
        ceiling,
        earlier[1] * jnp.exp(earlier[0] - ceiling) + later[1] * jnp.exp(later[0] - ceiling),
    )


def normalize(scores):
    row_ceiling = jnp.max(scores, axis=1)
    summed = jnp.sum(jnp.exp(scores - row_ceiling[:, None]), axis=1)
    ceiling_all, summed_all = joined((row_ceiling, summed), "orient", combine_totals)
    log_total = ceiling_all + jnp.log(summed_all)
    return jnp.exp(scores - log_total[:, None]).astype(jnp.bfloat16)


def local(images, projections, noise_weight, prior_score, routing, insert_kernel):
    classes, orient_local, pixels_local = projections.shape
    columns = classes * orient_local
    image_rows = images.shape[0]
    orient_count = lax.axis_size("orient")
    slab_count = lax.axis_size("slab")
    all_images = image_rows * orient_count
    widened = projections.astype(jnp.float32)
    weighted = (
        (widened * noise_weight[None, None, :]).astype(jnp.bfloat16).reshape(columns, pixels_local)
    )
    penalty = (-0.5 * jnp.sum(widened * widened * noise_weight[None, None, :], axis=2)).reshape(
        columns
    )
    block_rows = lax.all_gather(images, "orient", axis=0, tiled=True)
    block_scores = (
        lax.dot_general(
            block_rows, weighted, (((1,), (1,)), ((), ())), preferred_element_type=jnp.float32
        )
        + penalty[None, :]
    )
    partial_scores = block_scores
    stored = block_rows
    partial_scores, stored = (partial_scores, stored)
    prior_row = prior_score.reshape(columns)
    scores = lax.psum(partial_scores, "slab") + prior_row[None, :]
    weights = normalize(scores)
    block_count = pixels_local // PIECE
    weight_cube = weights.reshape(all_images, classes, orient_local)
    stored_blocks = stored.reshape(all_images, block_count, PIECE)
    slices = jnp.einsum(
        "iko,ipc->opkc", weight_cube, stored_blocks, preferred_element_type=jnp.float32
    ).astype(jnp.bfloat16)
    piece_count = orient_local * block_count
    slices = slices.reshape(piece_count, classes * PIECE)
    target = routing[0, :, :, 0].reshape(piece_count)
    voxel_index = routing[0, :, :, 1].reshape(piece_count)
    capacity = 2 * piece_count // slab_count
    owner_onehot = (target[:, None] == jnp.arange(slab_count, dtype=jnp.int32)[None, :]).astype(
        jnp.int32
    )
    before = jnp.cumsum(owner_onehot, axis=0) - owner_onehot
    slot_rank = jnp.sum(before * owner_onehot, axis=1)
    slot_index = target * capacity + slot_rank
    placing = (
        jnp.arange(slab_count * capacity, dtype=jnp.int32)[:, None] == slot_index[None, :]
    ).astype(jnp.int32)
    outgoing = jnp.dot(
        placing.astype(jnp.bfloat16), slices, preferred_element_type=jnp.float32
    ).astype(jnp.bfloat16)
    voxel_blocks = insert_kernel.shape[1] * orient_count
    filled = jnp.sum(placing, axis=1)
    slot_voxel = jnp.sum(placing * voxel_index[None, :], axis=1) + (1 - filled) * voxel_blocks
    arriving, arriving_voxel = (
        lax.all_to_all(
            outgoing.reshape(slab_count, capacity, classes * PIECE),
            "slab",
            split_axis=0,
            concat_axis=0,
            tiled=True,
        ),
        lax.all_to_all(
            slot_voxel.reshape(slab_count, capacity),
            "slab",
            split_axis=0,
            concat_axis=0,
            tiled=True,
        ),
    )
    received = arriving.reshape(slab_count * capacity, classes * PIECE)
    gathering = (
        jnp.arange(voxel_blocks, dtype=jnp.int32)[:, None]
        == arriving_voxel.reshape(slab_count * capacity)[None, :]
    ).astype(jnp.bfloat16)
    accumulated = jnp.dot(gathering, received, preferred_element_type=jnp.float32)
    own_blocks = lax.psum_scatter(accumulated, "orient", scatter_dimension=0, tiled=True)
    rounded = own_blocks.astype(jnp.bfloat16).reshape(own_blocks.shape[0], classes, PIECE)
    volume = jnp.einsum(
        "vkc,vce->vke", rounded, insert_kernel[0], preferred_element_type=jnp.float32
    )
    return volume[None]


def solution(mesh):
    placed = (
        P("orient", "slab"),
        P(None, "orient", "slab"),
        P("slab"),
        P(None, "orient"),
        P("slab", "orient", None, None),
        P("slab", "orient", None, None),
    )
    return jax.shard_map(
        local,
        mesh=mesh,
        in_specs=placed,
        out_specs=P("slab", "orient", None, None),
        check_vma=False,
    )
```

profile of v0, /device:TPU:6, one launch (start us, length us, event | category | flops | bytes accessed | tf_op | source)
XLA Modules:
  0.0 723.8 jit_solution(9435200211898309589)
XLA Ops:
  6.5 0.0 copy-start
  6.5 0.0 all-gather.4.cloned.1.call-start
  6.5 0.7 all-gather.4.cloned.1.call-update
  7.3 0.0 all-reduce.4.cloned.1.call-start
  7.3 2.0 fusion.2
  9.4 0.1 mul.88
  9.4 138.5 %all-gather.4.cloned.1.call-done = bf16[1024,2048]{1,0:T(8,128)(2,1)} async-done(((bf16[64,2048]{1,0:T(8,128)(2,1)}), bf16[1024,2048]{1,0:T(8,128)(2,1)}) %all-gather.4.cloned.1.call-update) | async-done | bytes 4194320 | tf_op jit(solution)/shard_map/all_gather | solution.py:47
  148.0 5.2 add_bitcast_fusion
  153.1 0.0 copy-start.2
  153.1 0.0 copy-start.3
  153.1 0.0 all-reduce.4.cloned.1.call-update
  153.1 0.7 copy-done.2
  153.9 0.1 copy.21
  153.9 0.1 eq.56
  154.0 0.1 reshape_squeeze.3
  154.1 1.7 reduce-window.6
  155.8 0.3 slice_reduce_fusion
  156.1 0.1 copy.24
  156.2 0.1 mul.77
  156.3 0.1 fusion.12
  156.4 1.4 convert_reduce_fusion
  157.8 0.7 add.57
  158.5 5.7 all-to-all-start
  164.2 0.0 copy-done.3
  164.2 0.1 add.61
  164.3 6.4 copy.25
  170.7 248.4 %all-reduce.4.cloned.1.call-done = f32[1024,384]{0,1:T(8,128)} async-done(((f32[1024,384]{0,1:T(8,128)}), f32[1024,384]{0,1:T(8,128)}) %all-reduce.4.cloned.1.call-update) | async-done | bytes 1572880 | tf_op jit(solution)/shard_map/psum | solution.py:58
  419.2 0.0 copy-start.1
  419.2 1.7 add_reduce_fusion
  420.9 0.2 copy-done.1
  421.0 0.3 exponential_reduce_fusion
  421.4 51.7 %all-gather.1 = f32[16384]{0:T(1024)S(1)} all-gather(f32[1024]{0:T(1024)S(1)} %exponential_reduce_fusion), channel_id=3, replica_groups=mesh['orient'=16,'slab'=32] {'orient'}, dimensions={0}, use_global_device_ids=true | all-gather | bytes 69632 | tf_op jit(solution)/shard_map/all_gather | solution.py:10
  473.1 45.5 %all-gather = f32[16384]{0:T(1024)S(1)} all-gather(f32[1024]{0:T(1024)S(1)} %add_reduce_fusion), channel_id=2, replica_groups=mesh['orient'=16,'slab'=32] {'orient'}, dimensions={0}, use_global_device_ids=true | all-gather | bytes 69632 | tf_op jit(solution)/shard_map/all_gather | solution.py:10
  518.6 0.8 while.12
  519.4 0.3 exponential_convert_fusion
  519.8 4.0 fusion.6
  523.8 1.0 copy.27
  524.8 3.9 convolution_convert_fusion
  528.7 0.0 all-to-all-done
  528.7 20.4 %all-to-all-start.1 = ((bf16[32,48,1024]{2,1,0:T(8,128)(2,1)}), bf16[32,48,1024]{2,1,0:T(8,128)(2,1)S(1)}, u32[]{:S(2)}, u32[]{:S(2)}) async-start(bf16[32,48,1024]{2,1,0:T(8,128)(2,1)} %bitcast.76), calls=%async_computation.1 | async-start | bytes 6291456 | tf_op jit(solution)/shard_map/all_to_all | solution.py:87
  549.2 1.3 dynamic-slice
  551.1 0.5 broadcast.61
  551.6 0.7 reduce.5
  552.3 0.1 eq.62
  552.4 67.7 %all-to-all-done.1 = bf16[32,48,1024]{2,1,0:T(8,128)(2,1)S(1)} async-done(((bf16[32,48,1024]{2,1,0:T(8,128)(2,1)}), bf16[32,48,1024]{2,1,0:T(8,128)(2,1)S(1)}, u32[]{:S(2)}, u32[]{:S(2)}) %all-to-all-start.1) | async-done | bytes 3145760 | tf_op jit(solution)/shard_map/all_to_all | solution.py:87
  620.1 0.7 fusion.7
  620.7 95.4 %all-reduce.5 = bf16[64,1024]{1,0:T(8,128)(2,1)S(1)} all-reduce(f32[64,1024]{1,0:T(8,128)S(1)} %fusion.7), channel_id=4, replica_groups=mesh['orient'=16,'slab'=32] {'orient'}, use_global_device_ids=true, to_apply=%region_11.12.clone | all-reduce | flops 65536 | bytes 393216
  716.2 0.0 copy-done
  716.2 0.8 convolution_bitcast_fusion
  (44 shorter events, 0.5 us)
Async XLA Ops:
  6.5 709.7 %copy-start = (bf16[1,4,128,128]{3,2,1,0:T(8,128)(2,1)S(1)}, bf16[1,4,128,128]{3,2,1,0:T(8,128)(2,1)}, u32[]{:S(2)}) copy-start(bf16[1,4,128,128]{3,2,1,0:T(8,128)(2,1)} %param.13) | copy-start | bytes 393220
  6.5 141.4 %all-gather.4.cloned.1.call-start = ((), (), s32[]{:S(2)}) async-start(), calls=%async_computation.2 | async-start | bytes 4456448 | tf_op jit(solution)/shard_map/all_gather | solution.py:47
  7.3 411.9 %all-reduce.4.cloned.1.call-start = ((), (), s32[]{:S(2)}) async-start(), calls=%async_computation.3 | async-start | bytes 3145728 | tf_op jit(solution)/shard_map/psum | solution.py:58
  153.1 0.7 copy-start.2
  153.1 11.1 %copy-start.3 = (f32[8,48]{1,0:T(8,128)S(1)}, f32[8,48]{1,0:T(8,128)}, u32[]{:S(2)}) copy-start(f32[8,48]{1,0:T(8,128)} %param.11) | copy-start | bytes 4612
  158.5 370.2 %all-to-all-start = ((s32[32,1,48]{2,1,0:T(1,128)}), s32[32,1,48]{2,1,0:T(1,128)S(1)}, u32[]{:S(2)}, u32[]{:S(2)}) async-start(s32[32,1,48]{2,1,0:T(1,128)} %add.57), calls=%async_computation | async-start | bytes 32768 | tf_op jit(solution)/shard_map/all_to_all | solution.py:94
  419.2 1.9 copy-start.1
  528.7 91.3 %all-to-all-start.1 = ((bf16[32,48,1024]{2,1,0:T(8,128)(2,1)}), bf16[32,48,1024]{2,1,0:T(8,128)(2,1)S(1)}, u32[]{:S(2)}, u32[]{:S(2)}) async-start(bf16[32,48,1024]{2,1,0:T(8,128)(2,1)} %bitcast.76), calls=%async_computation.1 | async-start | bytes 6291456 | tf_op jit(solution)/shard_map/all_to_all | solution.py:87
Sparse Core Ops, SparseCore 0:
  10.5 137.3 all-gather.3
  153.3 265.8 all-reduce.3
where the time goes:
time: 724 us
  waiting for transfers between devices  455 us (63%)
  blocking collectives  193 us (27%)
  starting transfers between devices  26.2 us (4%)
  matrix products  14.5 us (2%)
  between operations  14.2 us (2%)
  local copies, waits for them, and re-layouts  11.9 us (2%)
  other arithmetic  8.54 us (1%)
    psum x1, waiting for transfers between devices, local(): scores = lax.psum(partial_scores, 'slab') + prior_row[None, :]  248 us
    all_gather x1, waiting for transfers between devices, local(): block_rows = lax.all_gather(images, 'orient', axis=0, tiled=True)  139 us
    all_gather x2, blocking collectives, joined(): pieces = jax.tree.map(lambda part: lax.all_gather(part, axis), value)  97.2 us
    unnamed x1, blocking collectives  95.4 us
    all_to_all x1, waiting for transfers between devices, local(): lax.all_to_all(outgoing.reshape(slab_count, capacity, classes * PIECE), '...  67.7 us
    all_to_all x1, starting transfers between devices, local(): lax.all_to_all(outgoing.reshape(slab_count, capacity, classes * PIECE), '...  20.4 us
  transfers between devices with their start and end apart: 4, of which 3 were waited for; matrix products, arithmetic and copies ran while one was open for 4% of the time, Pallas kernels for 0%

commit v1 on v0

--- a/solution.py
+++ b/solution.py
@@ -44,7 +44,9 @@
     penalty = (-0.5 * jnp.sum(widened * widened * noise_weight[None, None, :], axis=2)).reshape(
         columns
     )
-    block_rows = lax.all_gather(images, "orient", axis=0, tiled=True)
+    block_rows = jnp.concatenate(
+        lax.all_to_all(jnp.stack([images] * lax.axis_size("orient")), "orient", 0, 0), axis=0
+    )
     block_scores = (
         lax.dot_general(
             block_rows, weighted, (((1,), (1,)), ((), ())), preferred_element_type=jnp.float32

time: 724 us -> 760 us (1.050)
  starting transfers between devices: 26.2 us -> 68.4 us
    all_gather x1 -> x0, waiting for transfers between devices: 139 us -> none  [local(): block_rows = lax.all_gather(images, 'orient', axis=0, tiled=True)]
    all_to_all x0 -> x1, waiting for transfers between devices: none -> 111 us  [local(): lax.all_to_all(jnp.stack([images] * lax.axis_size('orient')), 'orient', 0...]
    all_to_all x1, starting transfers between devices: 5.7 us -> 32.1 us  [local(): lax.all_to_all(slot_voxel.reshape(slab_count, capacity), 'slab', split_ax...]
    psum x1, waiting for transfers between devices: 248 us -> 269 us  [local(): scores = lax.psum(partial_scores, 'slab') + prior_row[None, :]]
    all_to_all x0 -> x1, starting transfers between devices: none -> 15.9 us  [local(): lax.all_to_all(jnp.stack([images] * lax.axis_size('orient')), 'orient', 0...]
  transfers between devices with their start and end apart: 4 -> 4, of which waited for: 3 -> 3; matrix products, arithmetic and copies ran while one was open for 4% -> 3% of each run, Pallas kernels for 0% -> 0%
where the time goes in v1:
time: 760 us; the launch traced here: 759 us
  waiting for transfers between devices  448 us (59%)
  blocking collectives  193 us (25%)
  starting transfers between devices  68.4 us (9%)
  local copies, waits for them, and re-layouts  14.5 us (2%)
  matrix products  14.5 us (2%)
  between operations  14.3 us (2%)
    psum x1, waiting for transfers between devices, local(): scores = lax.psum(partial_scores, 'slab') + prior_row[None, :]  269 us
    all_to_all x1, waiting for transfers between devices, local(): lax.all_to_all(jnp.stack([images] * lax.axis_size('orient')), 'orient', 0...  111 us
    all_gather x2, blocking collectives, joined(): pieces = jax.tree.map(lambda part: lax.all_gather(part, axis), value)  97.2 us
    unnamed x1, blocking collectives  95.4 us
    all_to_all x1, waiting for transfers between devices, local(): lax.all_to_all(outgoing.reshape(slab_count, capacity, classes * PIECE), '...  67.7 us
    all_to_all x1, starting transfers between devices, local(): lax.all_to_all(slot_voxel.reshape(slab_count, capacity), 'slab', split_ax...  32.1 us
    all_to_all x1, starting transfers between devices, local(): lax.all_to_all(outgoing.reshape(slab_count, capacity, classes * PIECE), '...  20.4 us
    all_to_all x1, starting transfers between devices, local(): lax.all_to_all(jnp.stack([images] * lax.axis_size('orient')), 'orient', 0...  15.9 us
  transfers between devices with their start and end apart: 4, of which 3 were waited for; matrix products, arithmetic and copies ran while one was open for 3% of the time, Pallas kernels for 0%

profile of v1, /device:TPU:6, one launch (start us, length us, event | category | flops | bytes accessed | tf_op | source)
XLA Modules:
  0.0 759.4 jit_solution(10104053410900078851)
XLA Ops:
  6.5 0.0 copy-start
  6.5 3.4 stack.2
  10.0 0.0 copy-start.2
  10.0 0.0 copy-start.4
  10.0 15.9 %all-to-all-start.1 = ((bf16[16,64,2048]{2,1,0:T(8,128)(2,1)}), bf16[16,64,2048]{2,1,0:T(8,128)(2,1)}, u32[]{:S(2)}, u32[]{:S(2)}) async-start(bf16[16,64,2048]{2,1,0:T(8,128)(2,1)} %stack.2), calls=%async_computation.1 | async-start | bytes 8388608 | tf_op jit(solution)/shard_map/all_to_all | solution.py:48
  25.8 0.0 all-reduce.4.cloned.1.call-start
  25.9 0.0 copy-done.2
  25.9 0.0 copy-done.4
  25.9 0.6 fusion.5
  26.6 0.1 mul.88
  26.6 111.0 %all-to-all-done.1 = bf16[16,64,2048]{2,1,0:T(8,128)(2,1)} async-done(((bf16[16,64,2048]{2,1,0:T(8,128)(2,1)}), bf16[16,64,2048]{2,1,0:T(8,128)(2,1)}, u32[]{:S(2)}, u32[]{:S(2)}) %all-to-all-start.1) | async-done | bytes 4194336 | tf_op jit(solution)/shard_map/all_to_all | solution.py:48
  137.7 5.2 add_bitcast_fusion
  142.8 0.0 copy-start.3
  142.8 0.0 copy-start.5
  142.8 0.0 all-reduce.4.cloned.1.call-update
  142.8 0.7 copy-done.3
  143.5 0.1 copy.19
  143.6 0.1 eq.56
  143.7 0.1 reshape_squeeze.3
  143.8 1.7 reduce-window.6
  145.5 0.3 slice_reduce_fusion
  145.8 0.1 copy.22
  145.9 0.1 mul.77
  146.0 0.1 fusion.20
  146.1 1.4 convert_reduce_fusion
  147.5 0.7 add.57
  148.2 32.1 %all-to-all-start = ((s32[32,1,48]{2,1,0:T(1,128)}), s32[32,1,48]{2,1,0:T(1,128)S(1)}, u32[]{:S(2)}, u32[]{:S(2)}) async-start(s32[32,1,48]{2,1,0:T(1,128)} %add.57), calls=%async_computation | async-start | bytes 32768 | tf_op jit(solution)/shard_map/all_to_all | solution.py:96
  180.3 0.0 copy-done.5
  180.3 0.1 add.61
  180.4 5.5 copy.27
  185.9 268.8 %all-reduce.4.cloned.1.call-done = f32[1024,384]{0,1:T(8,128)} async-done(((f32[1024,384]{0,1:T(8,128)}), f32[1024,384]{0,1:T(8,128)}) %all-reduce.4.cloned.1.call-update) | async-done | bytes 1572880 | tf_op jit(solution)/shard_map/psum | solution.py:60
  454.7 0.0 copy-start.1
  454.7 1.7 add_reduce_fusion
  456.4 0.2 copy-done.1
  456.6 0.3 exponential_reduce_fusion
  456.9 51.7 %all-gather.1 = f32[16384]{0:T(1024)S(1)} all-gather(f32[1024]{0:T(1024)S(1)} %exponential_reduce_fusion), channel_id=3, replica_groups=mesh['orient'=16,'slab'=32] {'orient'}, dimensions={0}, use_global_device_ids=true | all-gather | bytes 69632 | tf_op jit(solution)/shard_map/all_gather | solution.py:10
  508.6 45.5 %all-gather = f32[16384]{0:T(1024)S(1)} all-gather(f32[1024]{0:T(1024)S(1)} %add_reduce_fusion), channel_id=2, replica_groups=mesh['orient'=16,'slab'=32] {'orient'}, dimensions={0}, use_global_device_ids=true | all-gather | bytes 69632 | tf_op jit(solution)/shard_map/all_gather | solution.py:10
  554.2 0.8 while.12
  555.0 0.3 exponential_convert_fusion
  555.3 4.0 fusion.12
  559.3 1.0 copy.24
  560.3 3.9 convolution_convert_fusion
  564.3 0.0 all-to-all-done
  564.3 20.4 %all-to-all-start.2 = ((bf16[32,48,1024]{2,1,0:T(8,128)(2,1)}), bf16[32,48,1024]{2,1,0:T(8,128)(2,1)S(1)}, u32[]{:S(2)}, u32[]{:S(2)}) async-start(bf16[32,48,1024]{2,1,0:T(8,128)(2,1)} %bitcast.83), calls=%async_computation.2 | async-start | bytes 6291456 | tf_op jit(solution)/shard_map/all_to_all | solution.py:89
  584.7 1.3 dynamic-slice
  586.6 0.5 broadcast.63
  587.2 0.7 reduce.5
  587.9 0.1 eq.62
  587.9 67.7 %all-to-all-done.2 = bf16[32,48,1024]{2,1,0:T(8,128)(2,1)S(1)} async-done(((bf16[32,48,1024]{2,1,0:T(8,128)(2,1)}), bf16[32,48,1024]{2,1,0:T(8,128)(2,1)S(1)}, u32[]{:S(2)}, u32[]{:S(2)}) %all-to-all-start.2) | async-done | bytes 3145760 | tf_op jit(solution)/shard_map/all_to_all | solution.py:89
  655.6 0.7 fusion.15
  656.3 95.4 %all-reduce.5 = bf16[64,1024]{1,0:T(8,128)(2,1)S(1)} all-reduce(f32[64,1024]{1,0:T(8,128)S(1)} %fusion.15), channel_id=4, replica_groups=mesh['orient'=16,'slab'=32] {'orient'}, use_global_device_ids=true, to_apply=%region_11.12.clone | all-reduce | flops 65536 | bytes 393216
  751.7 0.0 copy-done
  751.8 0.8 convolution_bitcast_fusion
  (44 shorter events, 0.5 us)
Async XLA Ops:
  6.5 745.2 %copy-start = (bf16[1,4,128,128]{3,2,1,0:T(8,128)(2,1)S(1)}, bf16[1,4,128,128]{3,2,1,0:T(8,128)(2,1)}, u32[]{:S(2)}) copy-start(bf16[1,4,128,128]{3,2,1,0:T(8,128)(2,1)} %param.13) | copy-start | bytes 393220
  10.0 15.9 %copy-start.2 = (bf16[8,48,2048]{2,1,0:T(8,128)(2,1)S(1)}, bf16[8,48,2048]{2,1,0:T(8,128)(2,1)}, u32[]{:S(2)}) copy-start(bf16[8,48,2048]{2,1,0:T(8,128)(2,1)} %param.9) | copy-start | bytes 4718596
  10.0 15.9 %copy-start.4 = (f32[2048]{0:T(1024)S(1)}, f32[2048]{0:T(1024)}, u32[]{:S(2)}) copy-start(f32[2048]{0:T(1024)} %param.10) | copy-start | bytes 24580
  10.0 127.7 %all-to-all-start.1 = ((bf16[16,64,2048]{2,1,0:T(8,128)(2,1)}), bf16[16,64,2048]{2,1,0:T(8,128)(2,1)}, u32[]{:S(2)}, u32[]{:S(2)}) async-start(bf16[16,64,2048]{2,1,0:T(8,128)(2,1)} %stack.2), calls=%async_computation.1 | async-start | bytes 8388608 | tf_op jit(solution)/shard_map/all_to_all | solution.py:48
  25.8 428.9 %all-reduce.4.cloned.1.call-start = ((), (), s32[]{:S(2)}) async-start(), calls=%async_computation.3 | async-start | bytes 3145728 | tf_op jit(solution)/shard_map/psum | solution.py:60
  142.8 0.7 copy-start.3
  142.8 37.5 %copy-start.5 = (f32[8,48]{1,0:T(8,128)S(1)}, f32[8,48]{1,0:T(8,128)}, u32[]{:S(2)}) copy-start(f32[8,48]{1,0:T(8,128)} %param.11) | copy-start | bytes 4612
  148.2 416.1 %all-to-all-start = ((s32[32,1,48]{2,1,0:T(1,128)}), s32[32,1,48]{2,1,0:T(1,128)S(1)}, u32[]{:S(2)}, u32[]{:S(2)}) async-start(s32[32,1,48]{2,1,0:T(1,128)} %add.57), calls=%async_computation | async-start | bytes 32768 | tf_op jit(solution)/shard_map/all_to_all | solution.py:96
  454.7 1.9 copy-start.1
  564.3 91.3 %all-to-all-start.2 = ((bf16[32,48,1024]{2,1,0:T(8,128)(2,1)}), bf16[32,48,1024]{2,1,0:T(8,128)(2,1)S(1)}, u32[]{:S(2)}, u32[]{:S(2)}) async-start(bf16[32,48,1024]{2,1,0:T(8,128)(2,1)} %bitcast.83), calls=%async_computation.2 | async-start | bytes 6291456 | tf_op jit(solution)/shard_map/all_to_all | solution.py:89
Sparse Core Ops, SparseCore 0:
  143.0 311.7 all-reduce.3
